TPU v7x, 32 devices: a whole 2x2x4 slice. The times are simulated.
32 devices in a mesh: ctx: 8 (over z, x), head: 4 (over y, core).
Axes of the slice: x: 2, y: 2, z: 4, core: 2. Of those that a mesh axis runs over, the one named last changes fastest.
Arguments:
- queries: bfloat16 [1024, 32, 128], P('ctx', 'head'), may hold values from -14 to 14
- keys: bfloat16 [1024, 32, 128], P('ctx', 'head'), may hold values from -14 to 14
- values: bfloat16 [1024, 32, 128], P('ctx', 'head'), may hold values from -6 to 6
- gain: float32 [32, 128], P('head'), may hold values from 0.1 to 1.9
- doc_lengths: int32 [8], replicated, may hold values from 1 to 256, 1024 in all
- cotangent: bfloat16 [1024, 32, 128], P('ctx', 'head'), may hold values from -6 to 6
Outputs:
- mixed: bfloat16 [1024, 32, 128], P('ctx', 'head')
- query_grad: bfloat16 [1024, 32, 128], P('ctx', 'head')
- key_grad: bfloat16 [1024, 32, 128], P('ctx', 'head')
- value_grad: bfloat16 [1024, 32, 128], P('ctx', 'head')
All inputs are finite; a program needn't handle non-finite values.
Results may differ from a plain program's by a relative error of at most 0.0054.
Values may be sent and summed in bfloat16 or wider, within the bound.
A program may use at most 128 MiB of HBM per device.

v0:
```python
import jax
import jax.numpy as jnp
from jax import lax
from jax.sharding import PartitionSpec as P

SPAN = 2


neg_large = -1e30
norm_eps = 1e-06


def from_behind(x, axis, by):
    devices = lax.axis_size(axis)
    pairs = [(i, i + by) for i in range(devices) if 0 <= i + by < devices]
    return lax.ppermute(x, axis, pairs)


def carried_in(part, axis, combine, identity, reverse):
    count = lax.axis_size(axis)
    place = lax.axis_index(axis)
    ahead = count - 1 - place if reverse else place
    gathered = jax.tree.map(lambda a: lax.all_gather(a, axis), part)
    state = jax.tree.map(lambda a, e: jnp.zeros_like(a) + jnp.asarray(e, a.dtype), part, identity)

    def one(hop, state):
        source = count - 1 - hop if reverse else hop
        return combine(
            state, jax.tree.map(lambda a: lax.dynamic_index_in_dim(a, source, 0, False), gathered)
        )

    return lax.fori_loop(0, ahead, one, state)


def wide(form, left, right):
    return jnp.einsum(form, left, right, precision=lax.Precision.HIGHEST)


def narrow(form, left, right):
    return jnp.einsum(form, left, right, preferred_element_type=jnp.float32)


def doc_index(doc_lengths, positions):
    starts = jnp.cumsum(doc_lengths) - doc_lengths
    return jnp.sum((starts[None, :] <= positions[:, None]).astype(jnp.int32), axis=1) - 1


def one_doc(doc_lengths, position):
    return doc_index(doc_lengths, jnp.reshape(position, (1,)))[0]


def join_states(earlier, later):
    return (later[0] + (1.0 - later[1]) * earlier[0], jnp.maximum(earlier[1], later[1]))


def masked_scores(query_block, key_block, mask, scale):
    raw = narrow("thd,uhd->htu", query_block, key_block) * scale
    return jnp.where(mask[None], raw, neg_large)


def key_terms(dscores, weights, query_block, grad_block, scale):
    key_part = narrow("htu,thd->uhd", dscores, query_block) * scale
    value_part = narrow("htu,thd->uhd", weights, grad_block)
    return (key_part, value_part)


def per_device(queries, keys, values, gain, doc_lengths, cotangent):
    tile, heads, width = queries.shape
    features = heads * lax.axis_size("head") * width
    scale = width ** (-0.5)
    base = lax.axis_index("ctx") * tile
    offsets = jnp.arange(tile, dtype=jnp.int32)
    own_pos = base + offsets
    own_doc = doc_index(doc_lengths, own_pos)
    prev_doc = one_doc(doc_lengths, base - 1)
    next_doc = one_doc(doc_lengths, base + tile)
    pair = jnp.stack([keys, values])
    arrived = [from_behind(pair, "ctx", shift) for shift in range(SPAN, 0, -1)]
    key_tiles = [piece[0] for piece in arrived] + [keys]
    value_tiles = [piece[1] for piece in arrived] + [values]
    masks = []
    for position in range(SPAN + 1):
        key_pos = base - (SPAN - position) * tile + offsets
        key_doc = doc_index(doc_lengths, key_pos)
        masks.append(
            (own_doc[:, None] == key_doc[None, :]) & (key_pos[None, :] <= own_pos[:, None])
        )
    score_list = [
        masked_scores(queries, key_tiles[position], masks[position], scale)
        for position in range(SPAN + 1)
    ]
    top = score_list[0].max(axis=-1)
    for position in range(1, SPAN + 1):
        top = jnp.maximum(top, score_list[position].max(axis=-1))
    total = jnp.zeros((heads, tile), jnp.float32)
    for position in range(SPAN + 1):
        total = total + jnp.sum(jnp.exp(score_list[position] - top[..., None]), axis=-1)
    log_total = top + jnp.log(total)
    prob_list = []
    weight_list = []
    soft_out = jnp.zeros((tile, heads, width), jnp.float32)
    for position in range(SPAN + 1):
        probs = jnp.exp(score_list[position] - log_total[..., None])
        weights = probs.astype(jnp.bfloat16)
        prob_list.append(probs)
        weight_list.append(weights)
        soft_out = soft_out + narrow("htu,uhd->thd", weights, value_tiles[position])
    same_tile = masks[SPAN].astype(jnp.float32)
    carried_prev = (own_doc == prev_doc).astype(jnp.float32)
    carried_next = (own_doc == next_doc).astype(jnp.float32)
    keep_last = (own_doc == own_doc[tile - 1])[:, None, None]
    keep_first = (own_doc == own_doc[0])[:, None, None]
    reset_front = (prev_doc != own_doc[tile - 1]).astype(jnp.float32)
    reset_back = (next_doc != own_doc[0]).astype(jnp.float32)
    query_wide = queries.astype(jnp.float32)
    attend = (narrow("thd,uhd->htu", queries, keys) * same_tile).astype(jnp.bfloat16)
    local_state = narrow("uhd,uhe->hde", jnp.where(keep_last, keys, jnp.zeros_like(keys)), values)
    zero_state = jnp.zeros_like(local_state)
    incoming, front_flag = carried_in(
        (local_state, reset_front), "ctx", join_states, (zero_state, jnp.float32(0.0)), False
    )
    linear_out = (
        narrow("htu,uhd->thd", attend, values)
        + wide("thd,hde->the", query_wide, incoming) * carried_prev[:, None, None]
    )
    squares = lax.psum(jnp.sum(linear_out * linear_out, axis=(1, 2)), "head")
    inverse = lax.rsqrt(squares / features + norm_eps)
    mixed = (linear_out * inverse[:, None, None] * gain[None] + soft_out).astype(jnp.bfloat16)
    grad_wide = cotangent.astype(jnp.float32)
    weighted = grad_wide * gain[None]
    projection = lax.psum(jnp.sum(weighted * linear_out, axis=(1, 2)), "head")
    inner = (
        inverse[:, None, None] * weighted
        - linear_out * (inverse**3 * projection / features)[:, None, None]
    ).astype(jnp.bfloat16)
    row_dot = jnp.sum(grad_wide * soft_out, axis=-1).T
    query_soft = jnp.zeros((tile, heads, width), jnp.float32)
    dscore_list = []
    for position in range(SPAN + 1):
        dprobs = narrow("thd,uhd->htu", cotangent, value_tiles[position])
        dscores = (prob_list[position] * (dprobs - row_dot[..., None])).astype(jnp.bfloat16)
        query_soft = query_soft + narrow("htu,uhd->thd", dscores, key_tiles[position]) * scale
        dscore_list.append(dscores)
    inner_wide = inner.astype(jnp.float32)
    back = (narrow("thd,uhd->htu", inner, values) * same_tile).astype(jnp.bfloat16)
    query_linear = (
        narrow("htu,uhd->thd", back, keys)
        + wide("the,hde->thd", inner_wide, incoming) * carried_prev[:, None, None]
    )
    tile_sum = narrow(
        "thd,the->hde", jnp.where(keep_first, queries, jnp.zeros_like(queries)), inner
    )
    later, back_flag = carried_in(
        (tile_sum, reset_back), "ctx", join_states, (zero_state, jnp.float32(0.0)), True
    )
    key_linear = (
        narrow("htu,thd->uhd", back, queries)
        + wide("uhe,hde->uhd", values.astype(jnp.float32), later) * carried_next[:, None, None]
    )
    value_linear = (
        narrow("htu,the->uhe", attend, inner)
        + wide("uhd,hde->uhe", keys.astype(jnp.float32), later) * carried_next[:, None, None]
    )
    parts = [
        key_terms(dscore_list[position], weight_list[position], queries, cotangent, scale)
        for position in range(SPAN + 1)
    ]
    key_soft, value_soft = parts[SPAN]
    for shift in range(1, SPAN + 1):
        sent = jnp.stack([parts[SPAN - shift][0], parts[SPAN - shift][1]])
        returned = from_behind(sent.astype(jnp.bfloat16), "ctx", -shift).astype(sent.dtype)
        key_soft = key_soft + returned[0]
        value_soft = value_soft + returned[1]
    query_grad = (query_linear + query_soft).astype(jnp.bfloat16)
    key_grad = (key_linear + key_soft).astype(jnp.bfloat16)
    value_grad = (value_linear + value_soft).astype(jnp.bfloat16)
    return (mixed, query_grad, key_grad, value_grad)


def solution(mesh):
    placed = (
        P("ctx", "head", None),
        P("ctx", "head", None),
        P("ctx", "head", None),
        P("head", None),
        P(),
        P("ctx", "head", None),
    )
    return jax.shard_map(
        per_device,
        mesh=mesh,
        in_specs=placed,
        out_specs=(
            P("ctx", "head", None),
            P("ctx", "head", None),
            P("ctx", "head", None),
            P("ctx", "head", None),
        ),
        check_vma=False,
    )
```

profile of v0, /device:TPU:0, one launch (start us, length us, event | category | flops | bytes accessed | tf_op | source)
XLA Modules:
  0.0 254.4 jit_solution(11090392728132692730)
XLA Ops:
  7.3 0.9 reduce-window.9
  8.2 1.3 fusion.88
  11.5 1.3 compare_convert_fusion
  12.8 1.2 broadcast_select_fusion.1
  13.9 2.0 fusion.55
  16.0 1.1 copy_bitcast_fusion
  17.2 0.9 pad_maximum_fusion
  18.0 4.9 %collective-permute-start.1 = (bf16[2,128,8,128]{3,1,2,0:T(8,128)(2,1)}, bf16[2,128,8,128]{3,1,2,0:T(8,128)(2,1)S(1)}, u32[]{:S(2)}, u32[]{:S(2)}) collective-permute-start(bf16[2,128,8,128]{3,1,2,0:T(8,128)(2,1)} %pad_maximum_fusion), channel_id=1, source_target_pairs={{0,4},{4,8},{8,12},{12,16},{16,20},{20,24},{24,28},{1,5},{5,9},{9,... | collective-permute-start | bytes 1572872 | tf_op jit(solution)/shard_map/ppermute | solution.py:16
  22.9 3.5 %collective-permute-start = (bf16[2,128,8,128]{3,1,2,0:T(8,128)(2,1)}, bf16[2,128,8,128]{3,1,2,0:T(8,128)(2,1)S(1)}, u32[]{:S(2)}, u32[]{:S(2)}) collective-permute-start(bf16[2,128,8,128]{3,1,2,0:T(8,128)(2,1)} %pad_maximum_fusion), channel_id=1, source_target_pairs={{0,8},{4,12},{8,16},{12,20},{16,24},{20,28},{1,9},{5,13},{9,17},{1... | collective-permute-start | bytes 1572872 | tf_op jit(solution)/shard_map/ppermute | solution.py:16
  26.4 0.9 broadcast_select_fusion
  29.2 0.8 dynamic-update-slice.1
  30.0 0.8 dynamic-update-slice
  30.9 43.2 %all-reduce.2 = (f32[8]{0:T(128)S(1)}, f32[8]{0:T(128)S(1)}) all-reduce(f32[8]{0:T(128)S(1)} %dynamic-update-slice, f32[8]{0:T(128)S(1)} %dynamic-update-slice.1), channel_id=1, replica_groups=mesh['ctx'=8,'head'=4] {'ctx'}, use_global_device_ids=true, to_apply=%add | all-reduce | flops 16 | bytes 128
  76.2 1.2 fusion.58
  77.7 1.1 fusion.16
  78.8 28.5 %all-gather.5.cloned.1.call-done = f32[64,128,128]{2,1,0:T(8,128)} async-done(((f32[8,128,128]{2,1,0:T(8,128)}), f32[64,128,128]{2,1,0:T(8,128)}) %all-gather.5.cloned.1.call-update) | async-done | bytes 4194320 | tf_op jit(solution)/shard_map/all_gather | solution.py:23
  108.3 2.2 fusion.39
  110.5 5.6 %all-reduce.3 = (f32[128]{0:T(128)S(1)}, f32[128]{0:T(128)S(1)}) all-reduce(f32[128]{0:T(128)S(1)} %get-tuple-element.147, f32[128]{0:T(128)S(1)} %get-tuple-element.146), channel_id=1, replica_groups=mesh['ctx'=8,'head'=4] {'head'}, use_global_device_ids=true, to_apply=%region_6.7 | all-reduce | flops 256 | bytes 2048 | tf_op jit(solution)/shard_map/psum | solution.py:126
  116.2 2.2 fusion.38
  118.3 2.0 fusion.53
  120.9 1.1 convolution_bitcast_fusion
  122.0 1.8 copy.198
  123.8 1.3 fusion.25
  125.3 1.3 collective-permute-start.2
  127.3 1.3 collective-permute-start.3
  131.2 0.9 copy.199
  132.0 9.7 %collective-permute-done.2 = bf16[2,128,8,128]{3,1,2,0:T(8,128)(2,1)S(1)} collective-permute-done((bf16[2,128,8,128]{3,1,2,0:T(8,128)(2,1)S(1)}, bf16[2,128,8,128]{3,1,2,0:T(8,128)(2,1)S(1)}, u32[]{:S(2)}, u32[]{:S(2)}) %collective-permute-start.2) | collective-permute-done | bytes 524320 | tf_op jit(solution)/shard_map/ppermute | solution.py:16
  141.7 1.1 convert_element_type.115
  142.9 27.6 %collective-permute-done.3 = bf16[2,128,8,128]{3,1,2,0:T(8,128)(2,1)S(1)} collective-permute-done((bf16[2,128,8,128]{3,1,2,0:T(8,128)(2,1)S(1)}, bf16[2,128,8,128]{3,1,2,0:T(8,128)(2,1)S(1)}, u32[]{:S(2)}, u32[]{:S(2)}) %collective-permute-start.3) | collective-permute-done | bytes 524320 | tf_op jit(solution)/shard_map/ppermute | solution.py:16
  170.5 1.1 convert_element_type.116
  171.6 53.8 %all-gather.7.cloned.1.call-done = f32[64,128,128]{2,1,0:T(8,128)} async-done(((f32[8,128,128]{2,1,0:T(8,128)}), f32[64,128,128]{2,1,0:T(8,128)}) %all-gather.7.cloned.1.call-update) | async-done | bytes 4194320 | tf_op jit(solution)/shard_map/all_gather | solution.py:23
  225.4 18.4 %while.27 = (s32[]{:T(128)}, f32[8,128,128]{2,1,0:T(8,128)S(1)}, s32[]{:T(128)}, f32[8,8,128,128]{3,2,1,0:T(8,128)}, f32[8]{0:T(128)S(1)}, /*index=5*/s32[]{:T(128)}, s32[]{:T(128)}, s32[]{:T(128)}, s32[]{:T(128)}, f32[1]{0:T(128)}) while((s32[]{:T(128)}, f32[8,128,128]{2,1,0:T(8,128)S(1)}, s32[]{:T(128)}, f32[8,8,128,128]{3,2,1,0:T(8,128)}, ...), condition=%wide.region_20.21_spmd, body=%wide.region_19.20_spmd.sunk | while | flops 262151 | bytes 1573051 | solution.py:32
  225.4 0.7 dynamic_slice.35
  226.8 1.2 bitcast_add_fusion.5
  228.0 0.7 dynamic_slice.35
  229.4 1.2 bitcast_add_fusion.5
  230.7 0.7 dynamic_slice.35
  232.0 1.2 bitcast_add_fusion.5
  233.3 0.7 dynamic_slice.35
  234.7 1.2 bitcast_add_fusion.5
  235.9 0.7 dynamic_slice.35
  237.3 1.2 bitcast_add_fusion.5
  238.6 0.7 dynamic_slice.35
  239.9 1.2 bitcast_add_fusion.5
  241.2 0.7 dynamic_slice.35
  242.5 1.2 bitcast_add_fusion.5
  245.6 0.9 copy.200
  246.7 0.9 copy.201
  (79 shorter events, 10.7 us)
Async XLA Ops:
  7.2 21.5 %copy-start.14 = (u32[32]{0:T(128)S(1)}, u32[32]{0:T(128)}, u32[]{:S(2)}) copy-start(u32[32]{0:T(128)} %constant.115) | copy-start | bytes 388
  7.2 67.2 %copy-start.2 = (bf16[128,8,128]{2,1,0:T(8,128)(2,1)S(1)}, bf16[128,8,128]{2,1,0:T(8,128)(2,1)}, u32[]{:S(2)}) copy-start(bf16[128,8,128]{2,1,0:T(8,128)(2,1)} %param.11) | copy-start | bytes 786436
  7.2 67.0 %copy-start.3 = (bf16[128,8,128]{2,1,0:T(8,128)(2,1)S(1)}, bf16[128,8,128]{2,1,0:T(8,128)(2,1)}, u32[]{:S(2)}) copy-start(bf16[128,8,128]{2,1,0:T(8,128)(2,1)} %param.12) | copy-start | bytes 786436
  7.2 19.2 %copy-start.1 = (bf16[128,8,128]{2,1,0:T(8,128)(2,1)S(1)}, bf16[128,8,128]{2,1,0:T(8,128)(2,1)}, u32[]{:S(2)}) copy-start(bf16[128,8,128]{2,1,0:T(8,128)(2,1)} %param.10) | copy-start | bytes 786436
  7.2 100.1 %all-gather.5.cloned.1.call-start = ((), (), s32[]{:S(2)}) async-start(), calls=%async_computation | async-start | bytes 4718592 | tf_op jit(solution)/shard_map/all_gather | solution.py:23
  16.0 209.3 %all-gather.7.cloned.1.call-start = ((), (), s32[]{:S(2)}) async-start(), calls=%async_computation.1 | async-start | bytes 4718592 | tf_op jit(solution)/shard_map/all_gather | solution.py:23
  18.0 56.7 %collective-permute-start.1 = (bf16[2,128,8,128]{3,1,2,0:T(8,128)(2,1)}, bf16[2,128,8,128]{3,1,2,0:T(8,128)(2,1)S(1)}, u32[]{:S(2)}, u32[]{:S(2)}) collective-permute-start(bf16[2,128,8,128]{3,1,2,0:T(8,128)(2,1)} %pad_maximum_fusion), channel_id=1, source_target_pairs={{0,4},{4,8},{8,12},{12,16},{16,20},{20,24},{24,28},{1,5},{5,9},{9,... | collective-permute-start | bytes 1572872 | tf_op jit(solution)/shard_map/ppermute | solution.py:16
  22.9 52.2 %collective-permute-start = (bf16[2,128,8,128]{3,1,2,0:T(8,128)(2,1)}, bf16[2,128,8,128]{3,1,2,0:T(8,128)(2,1)S(1)}, u32[]{:S(2)}, u32[]{:S(2)}) collective-permute-start(bf16[2,128,8,128]{3,1,2,0:T(8,128)(2,1)} %pad_maximum_fusion), channel_id=1, source_target_pairs={{0,8},{4,12},{8,16},{12,20},{16,24},{20,28},{1,9},{5,13},{9,17},{1... | collective-permute-start | bytes 1572872 | tf_op jit(solution)/shard_map/ppermute | solution.py:16
  74.7 0.8 copy-start.9
  75.5 31.8 %copy-start.7 = (bf16[2,128,8,128]{3,1,2,0:T(8,128)(2,1)}, bf16[2,128,8,128]{3,1,2,0:T(8,128)(2,1)S(1)}, u32[]{:S(2)}) copy-start(bf16[2,128,8,128]{3,1,2,0:T(8,128)(2,1)S(1)} %collective-permute-done) | copy-start | bytes 1572868
  107.4 1.0 copy-start
  107.4 0.9 copy-start.13
  120.4 6.2 %copy-start.8 = (bf16[2,128,8,128]{3,1,2,0:T(8,128)(2,1)S(1)}, bf16[2,128,8,128]{3,1,2,0:T(8,128)(2,1)}, u32[]{:S(2)}) copy-start(bf16[2,128,8,128]{3,1,2,0:T(8,128)(2,1)} %copy-done.7) | copy-start | bytes 1572868
  120.9 8.0 %copy-start.10 = (bf16[2,128,8,128]{3,1,2,0:T(8,128)(2,1)S(1)}, bf16[2,128,8,128]{3,1,2,0:T(8,128)(2,1)}, u32[]{:S(2)}) copy-start(bf16[2,128,8,128]{3,1,2,0:T(8,128)(2,1)} %copy-done.9) | copy-start | bytes 1572868
  125.3 16.4 %collective-permute-start.2 = (bf16[2,128,8,128]{3,1,2,0:T(8,128)(2,1)S(1)}, bf16[2,128,8,128]{3,1,2,0:T(8,128)(2,1)S(1)}, u32[]{:S(2)}, u32[]{:S(2)}) collective-permute-start(bf16[2,128,8,128]{3,1,2,0:T(8,128)(2,1)S(1)} %pad_maximum_fusion.1), channel_id=1, source_target_pairs={{4,0},{8,4},{12,8},{16,12},{20,16},{24,20},{28,24},{5,1},{9,5},{13... | collective-permute-start | bytes 1572872 | tf_op jit(solution)/shard_map/ppermute | solution.py:16
  127.3 43.2 %collective-permute-start.3 = (bf16[2,128,8,128]{3,1,2,0:T(8,128)(2,1)S(1)}, bf16[2,128,8,128]{3,1,2,0:T(8,128)(2,1)S(1)}, u32[]{:S(2)}, u32[]{:S(2)}) collective-permute-start(bf16[2,128,8,128]{3,1,2,0:T(8,128)(2,1)S(1)} %pad_maximum_fusion.2), channel_id=1, source_target_pairs={{8,0},{12,4},{16,8},{20,12},{24,16},{28,20},{9,1},{13,5},{17,9},{2... | collective-permute-start | bytes 1572872 | tf_op jit(solution)/shard_map/ppermute | solution.py:16
  129.5 0.7 copy-start.11
  225.4 19.8 %copy-start.12 = (bf16[8,128,128]{1,2,0:T(8,128)(2,1)S(1)}, bf16[8,128,128]{1,2,0:T(8,128)(2,1)}, u32[]{:S(2)}) copy-start(bf16[8,128,128]{1,2,0:T(8,128)(2,1)} %copy-done.11) | copy-start | bytes 786436
  243.8 1.4 copy-start.4
  243.8 1.5 copy-start.5
  243.8 2.7 %copy-start.6 = (f32[128,8,128]{2,0,1:T(8,128)S(1)}, f32[128,8,128]{2,0,1:T(8,128)}, u32[]{:S(2)}) copy-start(f32[128,8,128]{2,0,1:T(8,128)} %convolution_bitcast_fusion) | copy-start | bytes 1572868
Sparse Core Ops, SparseCore 0:
  16.1 91.1 all-gather.4
  120.5 104.7 all-gather.6
where the time goes:
time: 255 us; the launch traced here: 254 us
  waiting for transfers between devices  120 us (47%)
  blocking collectives  48.9 us (19%)
  other arithmetic  20.2 us (8%)
  matrix products  18 us (7%)
  between operations  17.2 us (7%)
  local copies, waits for them, and re-layouts  14.6 us (6%)
  starting transfers between devices  11 us (4%)
  loops' own time  5.04 us (2%)
    all_gather x2, waiting for transfers between devices, carried_in(): gathered = jax.tree.map(lambda a: lax.all_gather(a, axis), part)  82.2 us
    unnamed x1, blocking collectives  43.2 us
    ppermute x4, waiting for transfers between devices, from_behind(): return lax.ppermute(x, axis, pairs)  37.3 us
    dot_general x25, matrix products, narrow(): return jnp.einsum(form, left, right, preferred_element_type=jnp.float32)  15.9 us
    ppermute x4, starting transfers between devices, from_behind(): return lax.ppermute(x, axis, pairs)  10.9 us
    add x7, other arithmetic, join_states(): later[0] + (1.0 - later[1]) * earlier[0]  8.72 us
    unnamed x40, local copies, waits for them, and re-layouts  8.1 us
    psum x1, blocking collectives, per_device(): squares = lax.psum(jnp.sum(linear_out * linear_out, axis=(1, 2)), 'head')  5.63 us
  transfers between devices with their start and end apart: 6, of which 4 were waited for; matrix products, arithmetic and copies ran while one was open for 8% of the time, Pallas kernels for 0%

commit v1 on v0

--- a/solution.py
+++ b/solution.py
@@ -1,6 +1,10 @@
+import functools
+
 import jax
 import jax.numpy as jnp
 from jax import lax
+from jax.experimental import pallas as pl
+from jax.experimental.pallas import tpu as pltpu
 from jax.sharding import PartitionSpec as P
 
 SPAN = 2
@@ -16,20 +20,27 @@
     return lax.ppermute(x, axis, pairs)
 
 
-def carried_in(part, axis, combine, identity, reverse):
+def carried_in(part, axis, combine, reverse):
     count = lax.axis_size(axis)
-    place = lax.axis_index(axis)
-    ahead = count - 1 - place if reverse else place
-    gathered = jax.tree.map(lambda a: lax.all_gather(a, axis), part)
-    state = jax.tree.map(lambda a, e: jnp.zeros_like(a) + jnp.asarray(e, a.dtype), part, identity)
-
-    def one(hop, state):
-        source = count - 1 - hop if reverse else hop
-        return combine(
-            state, jax.tree.map(lambda a: lax.dynamic_index_in_dim(a, source, 0, False), gathered)
-        )
-
-    return lax.fori_loop(0, ahead, one, state)
+    sign = -1 if reverse else 1
+
+    def moved(part, by):
+        return jax.tree.map(lambda a: from_behind(a, axis, sign * by), part)
+
+    state, by = moved(part, 1), 1
+    while by < count:
+        state = combine(moved(state, by), state)
+        by *= 2
+    return state
+
+
+def over_heads(x):
+    groups = lax.axis_size("head")
+    total = x
+    for by in range(1, groups):
+        pairs = [(i, (i + by) % groups) for i in range(groups)]
+        total = total + lax.ppermute(x, "head", pairs)
+    return total
 
 
 def wide(form, left, right):
@@ -41,7 +52,8 @@
 
 
 def doc_index(doc_lengths, positions):
-    starts = jnp.cumsum(doc_lengths) - doc_lengths
+    order = jnp.arange(doc_lengths.shape[0])
+    starts = jnp.sum(jnp.where(order[None, :] < order[:, None], doc_lengths[None, :], 0), axis=1)
     return jnp.sum((starts[None, :] <= positions[:, None]).astype(jnp.int32), axis=1) - 1
 
 
@@ -115,20 +127,19 @@
     query_wide = queries.astype(jnp.float32)
     attend = (narrow("thd,uhd->htu", queries, keys) * same_tile).astype(jnp.bfloat16)
     local_state = narrow("uhd,uhe->hde", jnp.where(keep_last, keys, jnp.zeros_like(keys)), values)
-    zero_state = jnp.zeros_like(local_state)
     incoming, front_flag = carried_in(
-        (local_state, reset_front), "ctx", join_states, (zero_state, jnp.float32(0.0)), False
+        (local_state, reset_front), "ctx", join_states, False
     )
     linear_out = (
         narrow("htu,uhd->thd", attend, values)
         + wide("thd,hde->the", query_wide, incoming) * carried_prev[:, None, None]
     )
-    squares = lax.psum(jnp.sum(linear_out * linear_out, axis=(1, 2)), "head")
+    squares = over_heads(jnp.sum(linear_out * linear_out, axis=(1, 2)))
     inverse = lax.rsqrt(squares / features + norm_eps)
     mixed = (linear_out * inverse[:, None, None] * gain[None] + soft_out).astype(jnp.bfloat16)
     grad_wide = cotangent.astype(jnp.float32)
     weighted = grad_wide * gain[None]
-    projection = lax.psum(jnp.sum(weighted * linear_out, axis=(1, 2)), "head")
+    projection = over_heads(jnp.sum(weighted * linear_out, axis=(1, 2)))
     inner = (
         inverse[:, None, None] * weighted
         - linear_out * (inverse**3 * projection / features)[:, None, None]
@@ -151,7 +162,7 @@
         "thd,the->hde", jnp.where(keep_first, queries, jnp.zeros_like(queries)), inner
     )
     later, back_flag = carried_in(
-        (tile_sum, reset_back), "ctx", join_states, (zero_state, jnp.float32(0.0)), True
+        (tile_sum, reset_back), "ctx", join_states, True
     )
     key_linear = (
         narrow("htu,thd->uhd", back, queries)
@@ -177,6 +188,423 @@
     return (mixed, query_grad, key_grad, value_grad)
 
 
+def mm(left, right, dims):
+    return lax.dot_general(left, right, (dims, ((), ())), preferred_element_type=jnp.float32)
+
+
+NT = ((1,), (1,))
+NN = ((1,), (0,))
+TN = ((0,), (0,))
+
+
+def block_kernel(
+    count, groups, features,
+    len_ref, q_ref, k_ref, v_ref, g_ref, do_ref,
+    mixed_ref, qg_ref, kg_ref, vg_ref,
+    wide_a, wide_b, q_own, qm_own, do_own, win, bias, keep, attend, lin, soft,
+    dq, dkv, part2, part1_tx, part2_tx, rx1, rx2, inner, t_tx, tx1, tz,
+    sq_acc, pj_acc, inv_b, coef_b, stat_tx, stat_rx,
+    kvz_s, kvz_r, kvx_s, kvx_r, pz_s, pz_r, px_s, px_r, tz_s, tz_r, tx_s, tx_r, st_s, st_r,
+):
+    heads, tile, width = q_own.shape
+    scale = width ** (-0.5)
+    bf = jnp.bfloat16
+    f32 = jnp.float32
+    me = lax.axis_index("ctx")
+    group = lax.axis_index("head")
+    odd = lax.rem(me, 2) == 1
+    even = lax.rem(me, 2) == 0
+    has_prev = me >= 2
+    has_next = me < count - 2
+    side = me + 1 - 2 * lax.rem(me, 2)
+
+    def remote(src, dst, send, recv, axis, to):
+        return pltpu.make_async_remote_copy(
+            src_ref=src, dst_ref=dst, send_sem=send, recv_sem=recv,
+            device_id={axis: to}, device_id_type=pl.DeviceIdType.MESH,
+        )
+
+    old, mid, own = pl.ds(0, tile), pl.ds(tile, tile), pl.ds(2 * tile, tile)
+
+    def kv_z(h):
+        return remote(win.at[h, :, own], win.at[h, :, old], kvz_s.at[h], kvz_r.at[h], "ctx", me + 2)
+
+    def kv_x_own(h):
+        return remote(win.at[h, :, own], win.at[h, :, mid], kvx_s.at[h], kvx_r.at[h], "ctx", side)
+
+    def kv_x_relay(h):
+        return remote(win.at[h, :, old], win.at[h, :, mid], kvx_s.at[h], kvx_r.at[h], "ctx", side)
+
+    def part_x(h):
+        return remote(part1_tx.at[h], rx1.at[h], px_s.at[h], px_r.at[h], "ctx", side)
+
+    def part_z(h):
+        return remote(part2_tx.at[h], rx2.at[h], pz_s.at[h], pz_r.at[h], "ctx", me - 2)
+
+    def state_z(h):
+        return remote(t_tx.at[h], tz.at[h], tz_s.at[h], tz_r.at[h], "ctx", me - 2)
+
+    def state_x_own(h):
+        return remote(t_tx.at[h], tx1.at[h], tx_s.at[h], tx_r.at[h], "ctx", side)
+
+    def state_x_relay(h):
+        return remote(tz.at[h], tx1.at[h], tx_s.at[h], tx_r.at[h], "ctx", side)
+
+    def stats(k):
+        return remote(
+            stat_tx, stat_rx.at[k - 1], st_s.at[k - 1], st_r.at[k - 1], "head",
+            lax.rem(group + k, groups),
+        )
+
+    def greet(axis, to):
+        pl.semaphore_signal(
+            barrier, inc=1, device_id={axis: to}, device_id_type=pl.DeviceIdType.MESH
+        )
+
+    barrier = pltpu.get_barrier_semaphore()
+    greet("ctx", side)
+    for k in range(1, groups):
+        greet("head", lax.rem(group + k, groups))
+
+    @pl.when(has_prev)
+    def _():
+        greet("ctx", me - 2)
+
+    @pl.when(has_next)
+    def _():
+        greet("ctx", me + 2)
+
+    wide_a[...] = k_ref[...].astype(f32).reshape(tile * heads, width)
+    wide_b[...] = v_ref[...].astype(f32).reshape(tile * heads, width)
+    for h in range(heads):
+        win[h, 0, 2 * tile:3 * tile, :] = wide_a[pl.ds(h, tile, stride=heads), :].astype(bf)
+        win[h, 1, 2 * tile:3 * tile, :] = wide_b[pl.ds(h, tile, stride=heads), :].astype(bf)
+
+    pl.semaphore_wait(barrier, groups + has_prev.astype(jnp.int32) + has_next.astype(jnp.int32))
+
+    def send_kv(h, carry):
+        @pl.when(has_next)
+        def _():
+            kv_z(h).start()
+
+        @pl.when(even)
+        def _():
+            kv_x_own(h).start()
+
+        return carry
+
+    lax.fori_loop(0, heads, send_kv, 0)
+
+    starts = []
+    running = jnp.int32(0)
+    for d in range(len_ref.shape[0]):
+        starts.append(running)
+        running = running + len_ref[d]
+    base = me * tile
+
+    def doc_of(position):
+        total = jnp.zeros_like(position)
+        for start in starts:
+            total = total + jnp.where(position >= start, 1, 0).astype(jnp.int32)
+        return total
+
+    rows = lax.broadcasted_iota(jnp.int32, (tile, tile), 0)
+    cols = lax.broadcasted_iota(jnp.int32, (tile, tile), 1)
+    own_pos = base + rows
+    own_doc = doc_of(own_pos)
+    for position in range(3):
+        key_pos = base - (2 - position) * tile + cols
+        allowed = (own_doc == doc_of(key_pos)) & (key_pos <= own_pos)
+        place = slice(position * tile, (position + 1) * tile)
+        bias[:, place] = jnp.where(allowed, 0.0, neg_large).astype(f32)
+        keep[:, place] = jnp.where(allowed, 1.0, 0.0).astype(f32)
+    first_doc = doc_of(base)
+    next_doc = doc_of(base + tile)
+    after_doc = doc_of(base + 2 * tile)
+    in_first = jnp.where(own_doc == first_doc, 1.0, 0.0).astype(f32)
+    in_next = jnp.where(own_doc == next_doc, 1.0, 0.0).astype(f32)
+    join = jnp.where(next_doc == after_doc, 1.0, 0.0).astype(f32)
+    is_even = jnp.where(even, 1.0, 0.0).astype(f32)
+
+    wide_a[...] = q_ref[...].astype(f32).reshape(tile * heads, width)
+    wide_b[...] = do_ref[...].astype(f32).reshape(tile * heads, width)
+    for h in range(heads):
+        q_h = wide_a[pl.ds(h, tile, stride=heads), :]
+        q_own[h] = q_h.astype(bf)
+        qm_own[h] = (q_h * in_first).astype(bf)
+        do_own[h] = wide_b[pl.ds(h, tile, stride=heads), :].astype(bf)
+    sq_acc[...] = jnp.zeros_like(sq_acc)
+    pj_acc[...] = jnp.zeros_like(pj_acc)
+
+    @pl.when(me < 2)
+    def _():
+        win[:, :, 0:tile, :] = jnp.zeros((heads, 2, tile, width), bf)
+
+    @pl.when(me == 0)
+    def _():
+        win[:, :, tile:2 * tile, :] = jnp.zeros((heads, 2, tile, width), bf)
+
+    @pl.when(me == 1)
+    def _():
+        rx1[...] = jnp.zeros_like(rx1)
+
+    @pl.when(me >= count - 2)
+    def _():
+        rx2[...] = jnp.zeros_like(rx2)
+        tz[...] = jnp.zeros_like(tz)
+
+    @pl.when(me == count - 1)
+    def _():
+        tx1[...] = jnp.zeros_like(tx1)
+
+    def pass_on(h):
+        part_x(h).wait_recv()
+        part2_tx[h] = (part2[h] + rx1[h].astype(f32)).astype(bf)
+        part_z(h).start()
+
+    def soft_step(h, carry):
+        @pl.when(has_prev)
+        def _():
+            kv_z(h).wait_recv()
+
+        @pl.when(odd & has_prev)
+        def _():
+            kv_x_relay(h).start()
+
+        @pl.when(odd | has_prev)
+        def _():
+            kv_x_own(h).wait_recv()
+
+        q_h, do_h = q_own[h], do_own[h]
+        k_w, v_w = win[h, 0], win[h, 1]
+        raw = mm(q_h, k_w, NT)
+        scores = raw * scale + bias[...]
+        top = jnp.max(scores, axis=-1, keepdims=True)
+        grown = jnp.exp(scores - top)
+        probs = grown * (1.0 / jnp.sum(grown, axis=-1, keepdims=True))
+        weights = probs.astype(bf)
+        soft_h = mm(weights, v_w, NN)
+        att = (raw * keep[...]).astype(bf)
+        lin_h = mm(att, v_w, NN)
+        grad = do_h.astype(f32)
+        row_dot = jnp.sum(grad * soft_h, axis=-1, keepdims=True)
+        dscores = (probs * (mm(do_h, v_w, NT) - row_dot)).astype(bf)
+        dq[h] = mm(dscores, k_w, NN) * scale
+        dk_w = mm(dscores, q_h, TN) * scale
+        dv_w = mm(weights, do_h, TN)
+        lin[h] = lin_h
+        soft[h] = soft_h
+        attend[h] = att[:, 2 * tile:]
+        dkv[h, 0] = dk_w[2 * tile:]
+        dkv[h, 1] = dv_w[2 * tile:]
+        part1_tx[h, 0] = dk_w[tile:2 * tile].astype(bf)
+        part1_tx[h, 1] = dv_w[tile:2 * tile].astype(bf)
+        sq_acc[...] += lin_h * lin_h
+        pj_acc[...] += grad * g_ref[pl.ds(h, 1), :] * lin_h
+
+        @pl.when(odd | has_prev)
+        def _():
+            part_x(h).start()
+
+        @pl.when(even & has_prev)
+        def _():
+            part2_tx[h, 0] = dk_w[:tile].astype(bf)
+            part2_tx[h, 1] = dv_w[:tile].astype(bf)
+            part_z(h).start()
+
+        @pl.when(odd & has_prev)
+        def _():
+            part2[h, 0] = dk_w[:tile]
+            part2[h, 1] = dv_w[:tile]
+
+        @pl.when(odd & has_prev & (h >= 2))
+        def _():
+            pass_on(jnp.maximum(h - 2, 0))
+
+        return carry
+
+    lax.fori_loop(0, heads, soft_step, 0)
+
+    sq_col = jnp.sum(sq_acc[...], axis=-1, keepdims=True)
+    pj_col = jnp.sum(pj_acc[...], axis=-1, keepdims=True)
+    flat = jnp.where(cols == 0, sq_col, jnp.where(cols == 1, pj_col, 0.0)).T
+    stat_tx[...] = flat[:8]
+    for k in range(1, groups):
+        stats(k).start()
+
+    @pl.when(odd & has_prev)
+    def _():
+        lax.fori_loop(heads - 2, heads, lambda h, c: (pass_on(h), c)[1], 0)
+
+    total = stat_tx[...]
+    for k in range(1, groups):
+        stats(k).wait_recv()
+        total = total + stat_rx[k - 1]
+    back_flat = jnp.concatenate([total, jnp.zeros((tile - 8, tile), f32)], axis=0).T
+    sq_sum = back_flat[:, 0:1]
+    pj_sum = back_flat[:, 1:2]
+    inverse = lax.rsqrt(sq_sum / features + norm_eps)
+    inv_b[...] = jnp.broadcast_to(inverse, (tile, width))
+    coef_b[...] = jnp.broadcast_to(inverse * inverse * inverse * pj_sum / features, (tile, width))
+
+    def state_step(h, carry):
+        weighted = do_own[h].astype(f32) * g_ref[pl.ds(h, 1), :]
+        inner_h = (inv_b[...] * weighted - lin[h] * coef_b[...]).astype(bf)
+        inner[h] = inner_h
+        t_tx[h] = mm(qm_own[h], inner_h, TN).astype(bf)
+
+        @pl.when(has_prev)
+        def _():
+            state_z(h).start()
+
+        @pl.when(odd)
+        def _():
+            state_x_own(h).start()
+
+        return carry
+
+    lax.fori_loop(0, heads, state_step, 0)
+
+    def local_step(h, carry):
+        @pl.when(has_next)
+        def _():
+            state_z(h).wait_recv()
+
+        @pl.when(even & has_next)
+        def _():
+            state_x_relay(h).start()
+
+        inner_h = inner[h]
+        back = (mm(inner_h, win[h, 1], NT) * keep[...]).astype(bf)
+        dq[h] += mm(back, win[h, 0], NN)
+        dkv[h, 0] += mm(back[:, 2 * tile:], q_own[h], TN)
+        dkv[h, 1] += mm(attend[h], inner_h, TN)
+        soft[h] += lin[h] * inv_b[...] * g_ref[pl.ds(h, 1), :]
+        return carry
+
+    lax.fori_loop(0, heads, local_step, 0)
+
+    for h in range(heads):
+        wide_a[pl.ds(h, tile, stride=heads), :] = soft[h]
+        wide_b[pl.ds(h, tile, stride=heads), :] = dq[h]
+    mixed_ref[...] = wide_a[...].reshape(tile, heads, width).astype(bf)
+    qg_ref[...] = wide_b[...].reshape(tile, heads, width).astype(bf)
+
+    def last_step(h, carry):
+        @pl.when(has_next)
+        def _():
+            part_z(h).wait_recv()
+
+        @pl.when(even)
+        def _():
+            part_x(h).wait_recv()
+
+        @pl.when(even | has_next)
+        def _():
+            state_x_own(h).wait_recv()
+
+        state = (tx1[h].astype(f32) + join * tz[h].astype(f32)).astype(bf)
+        got = rx1[h].astype(f32) * is_even + rx2[h].astype(f32)
+        dkv[h, 0] += got[0] + in_next * mm(win[h, 1, own, :], state, NT)
+        dkv[h, 1] += got[1] + in_next * mm(win[h, 0, own, :], state, NN)
+        return carry
+
+    lax.fori_loop(0, heads, last_step, 0)
+
+    for h in range(heads):
+        wide_a[pl.ds(h, tile, stride=heads), :] = dkv[h, 0]
+        wide_b[pl.ds(h, tile, stride=heads), :] = dkv[h, 1]
+    kg_ref[...] = wide_a[...].reshape(tile, heads, width).astype(bf)
+    vg_ref[...] = wide_b[...].reshape(tile, heads, width).astype(bf)
+
+    def drain(h, carry):
+        @pl.when(has_next)
+        def _():
+            kv_z(h).wait_send()
+
+        @pl.when(even | has_prev)
+        def _():
+            kv_x_own(h).wait_send()
+
+        @pl.when(odd | has_prev)
+        def _():
+            part_x(h).wait_send()
+
+        @pl.when(has_prev)
+        def _():
+            part_z(h).wait_send()
+            state_z(h).wait_send()
+
+        @pl.when(odd | has_next)
+        def _():
+            state_x_own(h).wait_send()
+
+        return carry
+
+    lax.fori_loop(0, heads, drain, 0)
+    for k in range(1, groups):
+        stats(k).wait_send()
+
+
+def in_window(queries, keys, values, gain, doc_lengths, cotangent):
+    tile, heads, width = queries.shape
+    count, groups = lax.axis_size("ctx"), lax.axis_size("head")
+    bf, f32 = jnp.bfloat16, jnp.float32
+    block = (heads, tile, width)
+    pair = (heads, 2, tile, width)
+    vmem = pl.BlockSpec(memory_space=pltpu.VMEM)
+    each = pltpu.SemaphoreType.DMA((heads,))
+    return pl.pallas_call(
+        functools.partial(block_kernel, count, groups, heads * groups * width),
+        out_shape=[jax.ShapeDtypeStruct(queries.shape, bf)] * 4,
+        in_specs=[pl.BlockSpec(memory_space=pltpu.SMEM)] + [vmem] * 5,
+        out_specs=[vmem] * 4,
+        scratch_shapes=[
+            pltpu.VMEM((tile * heads, width), f32),
+            pltpu.VMEM((tile * heads, width), f32),
+            pltpu.VMEM(block, bf),
+            pltpu.VMEM(block, bf),
+            pltpu.VMEM(block, bf),
+            pltpu.VMEM((heads, 2, 3 * tile, width), bf),
+            pltpu.VMEM((tile, 3 * tile), f32),
+            pltpu.VMEM((tile, 3 * tile), f32),
+            pltpu.VMEM((heads, tile, tile), bf),
+            pltpu.VMEM(block, f32),
+            pltpu.VMEM(block, f32),
+            pltpu.VMEM(block, f32),
+            pltpu.VMEM(pair, f32),
+            pltpu.VMEM(pair, f32),
+            pltpu.VMEM(pair, bf),
+            pltpu.VMEM(pair, bf),
+            pltpu.VMEM(pair, bf),
+            pltpu.VMEM(pair, bf),
+            pltpu.VMEM(block, bf),
+            pltpu.VMEM((heads, width, width), bf),
+            pltpu.VMEM((heads, width, width), bf),
+            pltpu.VMEM((heads, width, width), bf),
+            pltpu.VMEM((tile, width), f32),
+            pltpu.VMEM((tile, width), f32),
+            pltpu.VMEM((tile, width), f32),
+            pltpu.VMEM((tile, width), f32),
+            pltpu.VMEM((8, tile), f32),
+            pltpu.VMEM((groups - 1, 8, tile), f32),
+        ]
+        + [each] * 12
+        + [pltpu.SemaphoreType.DMA((groups - 1,))] * 2,
+        compiler_params=pltpu.CompilerParams(
+            collective_id=0, has_side_effects=True, vmem_limit_bytes=40 * 1024 * 1024
+        ),
+    )(doc_lengths, queries, keys, values, gain, cotangent)
+
+
+def dispatch(queries, keys, values, gain, doc_lengths, cotangent):
+    tile = queries.shape[0]
+    count = lax.axis_size("ctx")
+    if count * tile <= 4 * SPAN * tile and count % 2 == 0:
+        return tuple(in_window(queries, keys, values, gain, doc_lengths, cotangent))
+    return per_device(queries, keys, values, gain, doc_lengths, cotangent)
+
+
 def solution(mesh):
     placed = (
         P("ctx", "head", None),
@@ -187,7 +615,7 @@
         P("ctx", "head", None),
     )
     return jax.shard_map(
-        per_device,
+        dispatch,
         mesh=mesh,
         in_specs=placed,
         out_specs=(

time: 255 us -> 57.7 us (0.23)
  waiting for transfers between devices: 120 us -> 0 us
  blocking collectives: 48.9 us -> 0 us
  Pallas kernels: 0 us -> 48.8 us
  other arithmetic: 20.2 us -> 0 us
  matrix products: 18 us -> 0 us
  between operations: 17.2 us -> 0.66 us
  starting transfers between devices: 11 us -> 0 us
  local copies, waits for them, and re-layouts: 14.6 us -> 7.94 us
  loops' own time: 5.04 us -> 0 us
    all_gather x2 -> x0, waiting for transfers between devices: 82.2 us -> none  [carried_in(): gathered = jax.tree.map(lambda a: lax.all_gather(a, axis), part)]
    pallas_call x0 -> x1, Pallas kernels: none -> 48.8 us  [in_window(): pl.pallas_call(functools.partial(block_kernel, count, groups, heads * gro...]
    unnamed x1 -> x0, blocking collectives: 43.2 us -> none
    ppermute x4 -> x0, waiting for transfers between devices: 37.3 us -> none  [from_behind(): return lax.ppermute(x, axis, pairs)]
    dot_general x29 -> x0, matrix products: 18 us -> none  [the longest x25 15.9 us: narrow(): return jnp.einsum(form, left, right, preferred_element_type=jnp.float32)]
    ppermute x4 -> x0, starting transfers between devices: 10.9 us -> none  [from_behind(): return lax.ppermute(x, axis, pairs)]
    add x11 -> x0, other arithmetic: 8.75 us -> none  [the longest x7 8.72 us: join_states(): later[0] + (1.0 - later[1]) * earlier[0]]
    convert_element_type x5 -> x0, other arithmetic: 5.82 us -> none  [the longest x2 2.21 us: per_device(): from_behind(sent.astype(jnp.bfloat16), 'ctx', -shift).astype(sent.dtype)]
  transfers between devices with their start and end apart: 6 -> 0, of which waited for: 4 -> 0; matrix products, arithmetic and copies ran while one was open for 8% -> 0% of each run, Pallas kernels for 0% -> 0%
where the time goes in v1:
time: 57.7 us; the launch traced here: 57.4 us
  Pallas kernels  48.8 us (85%)
  local copies, waits for them, and re-layouts  7.94 us (14%)
  between operations  0.66 us (1%)
    pallas_call x1, Pallas kernels, in_window(): pl.pallas_call(functools.partial(block_kernel, count, groups, heads * gro...  48.8 us
    unnamed x16, local copies, waits for them, and re-layouts  7.94 us

profile of v1, /device:TPU:0, one launch (start us, length us, event | category | flops | bytes accessed | tf_op | source)
XLA Modules:
  0.0 57.4 jit_solution(9176781041879957670)
XLA Ops:
  0.6 0.0 copy-start
  0.6 0.9 %copy-done = bf16[128,8,128]{2,1,0:T(8,128)(2,1)S(1)} copy-done((bf16[128,8,128]{2,1,0:T(8,128)(2,1)S(1)}, bf16[128,8,128]{2,1,0:T(8,128)(2,1)}, u32[]{:S(2)}) %copy-start) | copy-done | bytes 262168
  1.6 0.0 copy-start.1
  1.6 0.9 %copy-done.1 = bf16[128,8,128]{2,1,0:T(8,128)(2,1)S(1)} copy-done((bf16[128,8,128]{2,1,0:T(8,128)(2,1)S(1)}, bf16[128,8,128]{2,1,0:T(8,128)(2,1)}, u32[]{:S(2)}) %copy-start.1) | copy-done | bytes 262168
  2.5 0.0 copy-start.2
  2.5 0.9 %copy-done.2 = bf16[128,8,128]{2,1,0:T(8,128)(2,1)S(1)} copy-done((bf16[128,8,128]{2,1,0:T(8,128)(2,1)S(1)}, bf16[128,8,128]{2,1,0:T(8,128)(2,1)}, u32[]{:S(2)}) %copy-start.2) | copy-done | bytes 262168
  3.5 0.0 copy-start.3
  3.5 0.9 %copy-done.3 = bf16[128,8,128]{2,1,0:T(8,128)(2,1)S(1)} copy-done((bf16[128,8,128]{2,1,0:T(8,128)(2,1)S(1)}, bf16[128,8,128]{2,1,0:T(8,128)(2,1)}, u32[]{:S(2)}) %copy-start.3) | copy-done | bytes 262168
  4.4 0.0 copy-start.4
  4.4 0.7 %copy-done.4 = f32[8,128]{1,0:T(8,128)S(1)} copy-done((f32[8,128]{1,0:T(8,128)S(1)}, f32[8,128]{1,0:T(8,128)}, u32[]{:S(2)}) %copy-start.4) | copy-done | bytes 4120
  5.1 0.0 copy-start.5
  5.1 0.7 %copy-done.5 = s32[8]{0:T(128)S(1)} copy-done((s32[8]{0:T(128)S(1)}, s32[8]{0:T(128)}, u32[]{:S(2)}) %copy-start.5) | copy-done | bytes 56
  5.8 48.8 %shard_map.93 = (bf16[128,8,128]{2,1,0:T(8,128)(2,1)S(1)}, bf16[128,8,128]{2,1,0:T(8,128)(2,1)S(1)}, bf16[128,8,128]{2,1,0:T(8,128)(2,1)S(1)}, bf16[128,8,128]{2,1,0:T(8,128)(2,1)S(1)}) custom-call(s32[8]{0:T(128)S(1)} %copy-done.5, bf16[128,8,128]{2,1,0:T(8,128)(2,1)S(1)} %copy-done, bf16[128,8,128]{2,1,0:T(8,128)(2,1)S(1)} %copy-done.1, ...), custom_call_target="tpu_custom_call" | custom-call | tf_op jit(solution)/shard_map/pallas_call | solution.py:557
  54.6 0.7 %copy.14 = bf16[128,8,128]{2,1,0:T(8,128)(2,1)} copy(bf16[128,8,128]{2,1,0:T(8,128)(2,1)S(1)} %get-tuple-element.8) | data formatting | bytes 524288
  55.3 0.7 %copy.15 = bf16[128,8,128]{2,1,0:T(8,128)(2,1)} copy(bf16[128,8,128]{2,1,0:T(8,128)(2,1)S(1)} %get-tuple-element.9) | data formatting | bytes 524288
  56.0 0.7 %copy.16 = bf16[128,8,128]{2,1,0:T(8,128)(2,1)} copy(bf16[128,8,128]{2,1,0:T(8,128)(2,1)S(1)} %get-tuple-element.10) | data formatting | bytes 524288
  56.7 0.7 %copy.17 = bf16[128,8,128]{2,1,0:T(8,128)(2,1)} copy(bf16[128,8,128]{2,1,0:T(8,128)(2,1)S(1)} %get-tuple-element.11) | data formatting | bytes 524288
Async XLA Ops:
  0.6 1.0 %copy-start = (bf16[128,8,128]{2,1,0:T(8,128)(2,1)S(1)}, bf16[128,8,128]{2,1,0:T(8,128)(2,1)}, u32[]{:S(2)}) copy-start(bf16[128,8,128]{2,1,0:T(8,128)(2,1)} %q_ref.1) | copy-start | bytes 786436
  1.6 0.9 %copy-start.1 = (bf16[128,8,128]{2,1,0:T(8,128)(2,1)S(1)}, bf16[128,8,128]{2,1,0:T(8,128)(2,1)}, u32[]{:S(2)}) copy-start(bf16[128,8,128]{2,1,0:T(8,128)(2,1)} %k_ref.1) | copy-start | bytes 786436
  2.5 0.9 %copy-start.2 = (bf16[128,8,128]{2,1,0:T(8,128)(2,1)S(1)}, bf16[128,8,128]{2,1,0:T(8,128)(2,1)}, u32[]{:S(2)}) copy-start(bf16[128,8,128]{2,1,0:T(8,128)(2,1)} %v_ref.1) | copy-start | bytes 786436
  3.5 0.9 %copy-start.3 = (bf16[128,8,128]{2,1,0:T(8,128)(2,1)S(1)}, bf16[128,8,128]{2,1,0:T(8,128)(2,1)}, u32[]{:S(2)}) copy-start(bf16[128,8,128]{2,1,0:T(8,128)(2,1)} %do_ref.1) | copy-start | bytes 786436
  4.4 0.7 %copy-start.4 = (f32[8,128]{1,0:T(8,128)S(1)}, f32[8,128]{1,0:T(8,128)}, u32[]{:S(2)}) copy-start(f32[8,128]{1,0:T(8,128)} %g_ref.1) | copy-start | bytes 12292
  5.1 0.7 %copy-start.5 = (s32[8]{0:T(128)S(1)}, s32[8]{0:T(128)}, u32[]{:S(2)}) copy-start(s32[8]{0:T(128)} %len_ref.1) | copy-start | bytes 100

commit v2 on v1

--- a/solution.py
+++ b/solution.py
@@ -199,8 +199,9 @@
 
 def block_kernel(
     count, groups, features,
-    len_ref, q_ref, k_ref, v_ref, g_ref, do_ref,
+    len_ref, q_hbm, k_hbm, v_hbm, g_hbm, do_hbm,
     mixed_ref, qg_ref, kg_ref, vg_ref,
+    q_ref, k_ref, v_ref, g_ref, do_ref, in_sem,
     wide_a, wide_b, q_own, qm_own, do_own, win, bias, keep, attend, lin, soft,
     dq, dkv, part2, part1_tx, part2_tx, rx1, rx2, inner, t_tx, tx1, tz,
     sq_acc, pj_acc, inv_b, coef_b, stat_tx, stat_rx,
@@ -217,6 +218,7 @@
     has_prev = me >= 2
     has_next = me < count - 2
     side = me + 1 - 2 * lax.rem(me, 2)
+    lag = heads // 2
 
     def remote(src, dst, send, recv, axis, to):
         return pltpu.make_async_remote_copy(
@@ -261,6 +263,14 @@
             barrier, inc=1, device_id={axis: to}, device_id_type=pl.DeviceIdType.MESH
         )
 
+    loads = [
+        pltpu.make_async_copy(source, target, in_sem.at[n])
+        for n, (source, target) in enumerate(
+            [(k_hbm, k_ref), (v_hbm, v_ref), (q_hbm, q_ref), (do_hbm, do_ref), (g_hbm, g_ref)]
+        )
+    ]
+    for load in loads:
+        load.start()
     barrier = pltpu.get_barrier_semaphore()
     greet("ctx", side)
     for k in range(1, groups):
@@ -274,6 +284,8 @@
     def _():
         greet("ctx", me + 2)
 
+    loads[0].wait()
+    loads[1].wait()
     wide_a[...] = k_ref[...].astype(f32).reshape(tile * heads, width)
     wide_b[...] = v_ref[...].astype(f32).reshape(tile * heads, width)
     for h in range(heads):
@@ -326,6 +338,8 @@
     join = jnp.where(next_doc == after_doc, 1.0, 0.0).astype(f32)
     is_even = jnp.where(even, 1.0, 0.0).astype(f32)
 
+    for load in loads[2:]:
+        load.wait()
     wide_a[...] = q_ref[...].astype(f32).reshape(tile * heads, width)
     wide_b[...] = do_ref[...].astype(f32).reshape(tile * heads, width)
     for h in range(heads):
@@ -417,9 +431,9 @@
             part2[h, 0] = dk_w[:tile]
             part2[h, 1] = dv_w[:tile]
 
-        @pl.when(odd & has_prev & (h >= 2))
-        def _():
-            pass_on(jnp.maximum(h - 2, 0))
+        @pl.when(odd & has_prev & (h >= lag))
+        def _():
+            pass_on(jnp.maximum(h - lag, 0))
 
         return carry
 
@@ -431,10 +445,6 @@
     stat_tx[...] = flat[:8]
     for k in range(1, groups):
         stats(k).start()
-
-    @pl.when(odd & has_prev)
-    def _():
-        lax.fori_loop(heads - 2, heads, lambda h, c: (pass_on(h), c)[1], 0)
 
     total = stat_tx[...]
     for k in range(1, groups):
@@ -460,6 +470,10 @@
         @pl.when(odd)
         def _():
             state_x_own(h).start()
+
+        @pl.when(odd & has_prev & (h >= heads - lag))
+        def _():
+            pass_on(jnp.maximum(h, heads - lag))
 
         return carry
 
@@ -557,9 +571,15 @@
     return pl.pallas_call(
         functools.partial(block_kernel, count, groups, heads * groups * width),
         out_shape=[jax.ShapeDtypeStruct(queries.shape, bf)] * 4,
-        in_specs=[pl.BlockSpec(memory_space=pltpu.SMEM)] + [vmem] * 5,
+        in_specs=[pl.BlockSpec(memory_space=pltpu.SMEM)] + [pl.BlockSpec(memory_space=pltpu.HBM)] * 5,
         out_specs=[vmem] * 4,
         scratch_shapes=[
+            pltpu.VMEM(queries.shape, bf),
+            pltpu.VMEM(queries.shape, bf),
+            pltpu.VMEM(queries.shape, bf),
+            pltpu.VMEM(gain.shape, f32),
+            pltpu.VMEM(queries.shape, bf),
+            pltpu.SemaphoreType.DMA((5,)),
             pltpu.VMEM((tile * heads, width), f32),
             pltpu.VMEM((tile * heads, width), f32),
             pltpu.VMEM(block, bf),
@@ -592,7 +612,7 @@
         + [each] * 12
         + [pltpu.SemaphoreType.DMA((groups - 1,))] * 2,
         compiler_params=pltpu.CompilerParams(
-            collective_id=0, has_side_effects=True, vmem_limit_bytes=40 * 1024 * 1024
+            collective_id=0, has_side_effects=True, vmem_limit_bytes=63 * 1024 * 1024
         ),
     )(doc_lengths, queries, keys, values, gain, cotangent)
 

time: 57.7 us -> 52.7 us (0.913)
  local copies, waits for them, and re-layouts: 7.94 us -> 4.5 us
  Pallas kernels: 48.8 us -> 47.3 us
    unnamed x16 -> x10, local copies, waits for them, and re-layouts: 7.94 us -> 4.5 us
    pallas_call x1, Pallas kernels: 48.8 us -> 47.3 us  [in_window(): pl.pallas_call(functools.partial(block_kernel, count, groups, heads * gro...]
where the time goes in v2:
time: 52.7 us; the launch traced here: 52.4 us
  Pallas kernels  47.3 us (90%)
  local copies, waits for them, and re-layouts  4.5 us (9%)
  between operations  0.65 us (1%)
    pallas_call x1, Pallas kernels, in_window(): pl.pallas_call(functools.partial(block_kernel, count, groups, heads * gro...  47.3 us
    unnamed x10, local copies, waits for them, and re-layouts  4.5 us

profile of v2, /device:TPU:0, one launch (start us, length us, event | category | flops | bytes accessed | tf_op | source)
XLA Modules:
  0.0 52.4 jit_solution(10779275453113303895)
XLA Ops:
  0.6 47.3 %shard_map.93 = (bf16[128,8,128]{2,1,0:T(8,128)(2,1)}, bf16[128,8,128]{2,1,0:T(8,128)(2,1)}, bf16[128,8,128]{2,1,0:T(8,128)(2,1)}, bf16[128,8,128]{2,1,0:T(8,128)(2,1)}) custom-call(s32[8]{0:T(128)} %len_ref.1, bf16[128,8,128]{2,1,0:T(8,128)(2,1)} %q_hbm.1, bf16[128,8,128]{2,1,0:T(8,128)(2,1)} %k_hbm.1, bf16[128,8,128]{2,1,0:T(8,128)(2,1)} %v_hbm.1, ...), custom_call_target="tpu_custom_call" | custom-call | tf_op jit(solution)/shard_map/pallas_call | solution.py:571
  47.9 0.0 copy-start.2
  47.9 1.7 %copy.14 = bf16[128,8,128]{2,1,0:T(8,128)(2,1)} copy(bf16[128,8,128]{2,1,0:T(8,128)(2,1)} %get-tuple-element.8) | data formatting | bytes 524288
  49.6 0.0 copy-done.2
  49.6 0.0 copy-start.1
  49.6 0.7 %copy.15 = bf16[128,8,128]{2,1,0:T(8,128)(2,1)} copy(bf16[128,8,128]{2,1,0:T(8,128)(2,1)S(1)} %copy-done.2) | data formatting | bytes 524288
  50.3 0.3 copy-done.1
  50.7 0.0 copy-start
  50.7 0.7 %copy.16 = bf16[128,8,128]{2,1,0:T(8,128)(2,1)} copy(bf16[128,8,128]{2,1,0:T(8,128)(2,1)S(1)} %copy-done.1) | data formatting | bytes 524288
  51.4 0.3 copy-done
  51.7 0.7 %copy.17 = bf16[128,8,128]{2,1,0:T(8,128)(2,1)} copy(bf16[128,8,128]{2,1,0:T(8,128)(2,1)S(1)} %copy-done) | data formatting | bytes 524288
Async XLA Ops:
  47.9 1.7 %copy-start.2 = (bf16[128,8,128]{2,1,0:T(8,128)(2,1)S(1)}, bf16[128,8,128]{2,1,0:T(8,128)(2,1)}, u32[]{:S(2)}) copy-start(bf16[128,8,128]{2,1,0:T(8,128)(2,1)} %get-tuple-element.9) | copy-start | bytes 786436
  49.6 1.0 %copy-start.1 = (bf16[128,8,128]{2,1,0:T(8,128)(2,1)S(1)}, bf16[128,8,128]{2,1,0:T(8,128)(2,1)}, u32[]{:S(2)}) copy-start(bf16[128,8,128]{2,1,0:T(8,128)(2,1)} %get-tuple-element.10) | copy-start | bytes 786436
  50.7 1.0 %copy-start = (bf16[128,8,128]{2,1,0:T(8,128)(2,1)S(1)}, bf16[128,8,128]{2,1,0:T(8,128)(2,1)}, u32[]{:S(2)}) copy-start(bf16[128,8,128]{2,1,0:T(8,128)(2,1)} %get-tuple-element.11) | copy-start | bytes 786436

commit v3 on v2

--- a/solution.py
+++ b/solution.py
@@ -202,10 +202,10 @@
     len_ref, q_hbm, k_hbm, v_hbm, g_hbm, do_hbm,
     mixed_ref, qg_ref, kg_ref, vg_ref,
     q_ref, k_ref, v_ref, g_ref, do_ref, in_sem,
-    wide_a, wide_b, q_own, qm_own, do_own, win, bias, keep, attend, lin, soft,
-    dq, dkv, part2, part1_tx, part2_tx, rx1, rx2, inner, t_tx, tx1, tz,
+    wide_a, wide_b, q_own, do_own, win, bias, keep, attend, lin, soft,
+    dq, dkv, part1_tx, part2_tx, rx1, rx2,
     sq_acc, pj_acc, inv_b, coef_b, stat_tx, stat_rx,
-    kvz_s, kvz_r, kvx_s, kvx_r, pz_s, pz_r, px_s, px_r, tz_s, tz_r, tx_s, tx_r, st_s, st_r,
+    kvz_s, kvz_r, kvx_s, kvx_r, pz_s, pz_r, px_s, px_r, st_s, st_r,
 ):
     heads, tile, width = q_own.shape
     scale = width ** (-0.5)
@@ -218,7 +218,7 @@
     has_prev = me >= 2
     has_next = me < count - 2
     side = me + 1 - 2 * lax.rem(me, 2)
-    lag = heads // 2
+    lag = 2
 
     def remote(src, dst, send, recv, axis, to):
         return pltpu.make_async_remote_copy(
@@ -242,15 +242,6 @@
 
     def part_z(h):
         return remote(part2_tx.at[h], rx2.at[h], pz_s.at[h], pz_r.at[h], "ctx", me - 2)
-
-    def state_z(h):
-        return remote(t_tx.at[h], tz.at[h], tz_s.at[h], tz_r.at[h], "ctx", me - 2)
-
-    def state_x_own(h):
-        return remote(t_tx.at[h], tx1.at[h], tx_s.at[h], tx_r.at[h], "ctx", side)
-
-    def state_x_relay(h):
-        return remote(tz.at[h], tx1.at[h], tx_s.at[h], tx_r.at[h], "ctx", side)
 
     def stats(k):
         return remote(
@@ -330,12 +321,6 @@
         place = slice(position * tile, (position + 1) * tile)
         bias[:, place] = jnp.where(allowed, 0.0, neg_large).astype(f32)
         keep[:, place] = jnp.where(allowed, 1.0, 0.0).astype(f32)
-    first_doc = doc_of(base)
-    next_doc = doc_of(base + tile)
-    after_doc = doc_of(base + 2 * tile)
-    in_first = jnp.where(own_doc == first_doc, 1.0, 0.0).astype(f32)
-    in_next = jnp.where(own_doc == next_doc, 1.0, 0.0).astype(f32)
-    join = jnp.where(next_doc == after_doc, 1.0, 0.0).astype(f32)
     is_even = jnp.where(even, 1.0, 0.0).astype(f32)
 
     for load in loads[2:]:
@@ -345,7 +330,6 @@
     for h in range(heads):
         q_h = wide_a[pl.ds(h, tile, stride=heads), :]
         q_own[h] = q_h.astype(bf)
-        qm_own[h] = (q_h * in_first).astype(bf)
         do_own[h] = wide_b[pl.ds(h, tile, stride=heads), :].astype(bf)
     sq_acc[...] = jnp.zeros_like(sq_acc)
     pj_acc[...] = jnp.zeros_like(pj_acc)
@@ -365,15 +349,10 @@
     @pl.when(me >= count - 2)
     def _():
         rx2[...] = jnp.zeros_like(rx2)
-        tz[...] = jnp.zeros_like(tz)
-
-    @pl.when(me == count - 1)
-    def _():
-        tx1[...] = jnp.zeros_like(tx1)
 
     def pass_on(h):
         part_x(h).wait_recv()
-        part2_tx[h] = (part2[h] + rx1[h].astype(f32)).astype(bf)
+        part2_tx[h] = (dkv[h, :, 0:tile, :] + rx1[h].astype(f32)).astype(bf)
         part_z(h).start()
 
     def soft_step(h, carry):
@@ -404,36 +383,13 @@
         row_dot = jnp.sum(grad * soft_h, axis=-1, keepdims=True)
         dscores = (probs * (mm(do_h, v_w, NT) - row_dot)).astype(bf)
         dq[h] = mm(dscores, k_w, NN) * scale
-        dk_w = mm(dscores, q_h, TN) * scale
-        dv_w = mm(weights, do_h, TN)
+        dkv[h, 0] = mm(dscores, q_h, TN) * scale
+        dkv[h, 1] = mm(weights, do_h, TN)
         lin[h] = lin_h
         soft[h] = soft_h
-        attend[h] = att[:, 2 * tile:]
-        dkv[h, 0] = dk_w[2 * tile:]
-        dkv[h, 1] = dv_w[2 * tile:]
-        part1_tx[h, 0] = dk_w[tile:2 * tile].astype(bf)
-        part1_tx[h, 1] = dv_w[tile:2 * tile].astype(bf)
+        attend[h] = att
         sq_acc[...] += lin_h * lin_h
         pj_acc[...] += grad * g_ref[pl.ds(h, 1), :] * lin_h
-
-        @pl.when(odd | has_prev)
-        def _():
-            part_x(h).start()
-
-        @pl.when(even & has_prev)
-        def _():
-            part2_tx[h, 0] = dk_w[:tile].astype(bf)
-            part2_tx[h, 1] = dv_w[:tile].astype(bf)
-            part_z(h).start()
-
-        @pl.when(odd & has_prev)
-        def _():
-            part2[h, 0] = dk_w[:tile]
-            part2[h, 1] = dv_w[:tile]
-
-        @pl.when(odd & has_prev & (h >= lag))
-        def _():
-            pass_on(jnp.maximum(h - lag, 0))
 
         return carry
 
@@ -457,46 +413,37 @@
     inv_b[...] = jnp.broadcast_to(inverse, (tile, width))
     coef_b[...] = jnp.broadcast_to(inverse * inverse * inverse * pj_sum / features, (tile, width))
 
-    def state_step(h, carry):
+    def linear_step(h, carry):
         weighted = do_own[h].astype(f32) * g_ref[pl.ds(h, 1), :]
-        inner_h = (inv_b[...] * weighted - lin[h] * coef_b[...]).astype(bf)
-        inner[h] = inner_h
-        t_tx[h] = mm(qm_own[h], inner_h, TN).astype(bf)
-
-        @pl.when(has_prev)
-        def _():
-            state_z(h).start()
-
-        @pl.when(odd)
-        def _():
-            state_x_own(h).start()
-
-        @pl.when(odd & has_prev & (h >= heads - lag))
-        def _():
-            pass_on(jnp.maximum(h, heads - lag))
-
+        lin_h = lin[h]
+        inner_h = (inv_b[...] * weighted - lin_h * coef_b[...]).astype(bf)
+        back = (mm(inner_h, win[h, 1], NT) * keep[...]).astype(bf)
+        dkv[h, 0] += mm(back, q_own[h], TN)
+        dkv[h, 1] += mm(attend[h], inner_h, TN)
+
+        @pl.when(odd | has_prev)
+        def _():
+            part1_tx[h] = dkv[h, :, tile:2 * tile, :].astype(bf)
+            part_x(h).start()
+
+        @pl.when(even & has_prev)
+        def _():
+            part2_tx[h] = dkv[h, :, 0:tile, :].astype(bf)
+            part_z(h).start()
+
+        @pl.when(odd & has_prev & (h >= lag))
+        def _():
+            pass_on(jnp.maximum(h - lag, 0))
+
+        dq[h] += mm(back, win[h, 0], NN)
+        soft[h] += lin_h * inv_b[...] * g_ref[pl.ds(h, 1), :]
         return carry
 
-    lax.fori_loop(0, heads, state_step, 0)
-
-    def local_step(h, carry):
-        @pl.when(has_next)
-        def _():
-            state_z(h).wait_recv()
-
-        @pl.when(even & has_next)
-        def _():
-            state_x_relay(h).start()
-
-        inner_h = inner[h]
-        back = (mm(inner_h, win[h, 1], NT) * keep[...]).astype(bf)
-        dq[h] += mm(back, win[h, 0], NN)
-        dkv[h, 0] += mm(back[:, 2 * tile:], q_own[h], TN)
-        dkv[h, 1] += mm(attend[h], inner_h, TN)
-        soft[h] += lin[h] * inv_b[...] * g_ref[pl.ds(h, 1), :]
-        return carry
-
-    lax.fori_loop(0, heads, local_step, 0)
+    lax.fori_loop(0, heads, linear_step, 0)
+
+    @pl.when(odd & has_prev)
+    def _():
+        lax.fori_loop(heads - lag, heads, lambda h, c: (pass_on(h), c)[1], 0)
 
     for h in range(heads):
         wide_a[pl.ds(h, tile, stride=heads), :] = soft[h]
@@ -513,21 +460,15 @@
         def _():
             part_x(h).wait_recv()
 
-        @pl.when(even | has_next)
-        def _():
-            state_x_own(h).wait_recv()
-
-        state = (tx1[h].astype(f32) + join * tz[h].astype(f32)).astype(bf)
         got = rx1[h].astype(f32) * is_even + rx2[h].astype(f32)
-        dkv[h, 0] += got[0] + in_next * mm(win[h, 1, own, :], state, NT)
-        dkv[h, 1] += got[1] + in_next * mm(win[h, 0, own, :], state, NN)
+        dkv[h, :, 2 * tile:3 * tile, :] += got
         return carry
 
     lax.fori_loop(0, heads, last_step, 0)
 
     for h in range(heads):
-        wide_a[pl.ds(h, tile, stride=heads), :] = dkv[h, 0]
-        wide_b[pl.ds(h, tile, stride=heads), :] = dkv[h, 1]
+        wide_a[pl.ds(h, tile, stride=heads), :] = dkv[h, 0, 2 * tile:3 * tile, :]
+        wide_b[pl.ds(h, tile, stride=heads), :] = dkv[h, 1, 2 * tile:3 * tile, :]
     kg_ref[...] = wide_a[...].reshape(tile, heads, width).astype(bf)
     vg_ref[...] = wide_b[...].reshape(tile, heads, width).astype(bf)
 
@@ -547,11 +488,6 @@
         @pl.when(has_prev)
         def _():
             part_z(h).wait_send()
-            state_z(h).wait_send()
-
-        @pl.when(odd | has_next)
-        def _():
-            state_x_own(h).wait_send()
 
         return carry
 
@@ -584,24 +520,18 @@
             pltpu.VMEM((tile * heads, width), f32),
             pltpu.VMEM(block, bf),
             pltpu.VMEM(block, bf),
-            pltpu.VMEM(block, bf),
             pltpu.VMEM((heads, 2, 3 * tile, width), bf),
             pltpu.VMEM((tile, 3 * tile), f32),
             pltpu.VMEM((tile, 3 * tile), f32),
-            pltpu.VMEM((heads, tile, tile), bf),
+            pltpu.VMEM((heads, tile, 3 * tile), bf),
             pltpu.VMEM(block, f32),
             pltpu.VMEM(block, f32),
             pltpu.VMEM(block, f32),
-            pltpu.VMEM(pair, f32),
-            pltpu.VMEM(pair, f32),
+            pltpu.VMEM((heads, 2, 3 * tile, width), f32),
             pltpu.VMEM(pair, bf),
             pltpu.VMEM(pair, bf),
             pltpu.VMEM(pair, bf),
             pltpu.VMEM(pair, bf),
-            pltpu.VMEM(block, bf),
-            pltpu.VMEM((heads, width, width), bf),
-            pltpu.VMEM((heads, width, width), bf),
-            pltpu.VMEM((heads, width, width), bf),
             pltpu.VMEM((tile, width), f32),
             pltpu.VMEM((tile, width), f32),
             pltpu.VMEM((tile, width), f32),
@@ -609,7 +539,7 @@
             pltpu.VMEM((8, tile), f32),
             pltpu.VMEM((groups - 1, 8, tile), f32),
         ]
-        + [each] * 12
+        + [each] * 8
         + [pltpu.SemaphoreType.DMA((groups - 1,))] * 2,
         compiler_params=pltpu.CompilerParams(
             collective_id=0, has_side_effects=True, vmem_limit_bytes=63 * 1024 * 1024

time: 52.7 us -> 47.8 us (0.907)
  the two profiles are of different devices: /device:TPU:0 before, /device:TPU:18 now
where the time goes in v3:
time: 47.8 us; the launch traced here: 47.6 us
  Pallas kernels  42.5 us (89%)
  local copies, waits for them, and re-layouts  4.5 us (9%)
  between operations  0.65 us (1%)
    pallas_call x1, Pallas kernels, in_window(): pl.pallas_call(functools.partial(block_kernel, count, groups, heads * gro...  42.5 us
    unnamed x10, local copies, waits for them, and re-layouts  4.5 us

profile of v3, /device:TPU:18, one launch (start us, length us, event | category | flops | bytes accessed | tf_op | source)
XLA Modules:
  0.0 47.6 jit_solution(13756112561796648467)
XLA Ops:
  0.6 42.5 %shard_map.93 = (bf16[128,8,128]{2,1,0:T(8,128)(2,1)}, bf16[128,8,128]{2,1,0:T(8,128)(2,1)}, bf16[128,8,128]{2,1,0:T(8,128)(2,1)}, bf16[128,8,128]{2,1,0:T(8,128)(2,1)}) custom-call(s32[8]{0:T(128)} %len_ref.1, bf16[128,8,128]{2,1,0:T(8,128)(2,1)} %q_hbm.1, bf16[128,8,128]{2,1,0:T(8,128)(2,1)} %k_hbm.1, bf16[128,8,128]{2,1,0:T(8,128)(2,1)} %v_hbm.1, ...), custom_call_target="tpu_custom_call" | custom-call | tf_op jit(solution)/shard_map/pallas_call | solution.py:507
  43.1 0.0 copy-start.2
  43.1 1.7 %copy.14 = bf16[128,8,128]{2,1,0:T(8,128)(2,1)} copy(bf16[128,8,128]{2,1,0:T(8,128)(2,1)} %get-tuple-element.8) | data formatting | bytes 524288
  44.8 0.0 copy-done.2
  44.8 0.0 copy-start.1
  44.8 0.7 %copy.15 = bf16[128,8,128]{2,1,0:T(8,128)(2,1)} copy(bf16[128,8,128]{2,1,0:T(8,128)(2,1)S(1)} %copy-done.2) | data formatting | bytes 524288
  45.5 0.3 copy-done.1
  45.9 0.0 copy-start
  45.9 0.7 %copy.16 = bf16[128,8,128]{2,1,0:T(8,128)(2,1)} copy(bf16[128,8,128]{2,1,0:T(8,128)(2,1)S(1)} %copy-done.1) | data formatting | bytes 524288
  46.6 0.3 copy-done
  46.9 0.7 %copy.17 = bf16[128,8,128]{2,1,0:T(8,128)(2,1)} copy(bf16[128,8,128]{2,1,0:T(8,128)(2,1)S(1)} %copy-done) | data formatting | bytes 524288
Async XLA Ops:
  43.1 1.7 %copy-start.2 = (bf16[128,8,128]{2,1,0:T(8,128)(2,1)S(1)}, bf16[128,8,128]{2,1,0:T(8,128)(2,1)}, u32[]{:S(2)}) copy-start(bf16[128,8,128]{2,1,0:T(8,128)(2,1)} %get-tuple-element.9) | copy-start | bytes 786436
  44.8 1.0 %copy-start.1 = (bf16[128,8,128]{2,1,0:T(8,128)(2,1)S(1)}, bf16[128,8,128]{2,1,0:T(8,128)(2,1)}, u32[]{:S(2)}) copy-start(bf16[128,8,128]{2,1,0:T(8,128)(2,1)} %get-tuple-element.10) | copy-start | bytes 786436
  45.9 1.0 %copy-start = (bf16[128,8,128]{2,1,0:T(8,128)(2,1)S(1)}, bf16[128,8,128]{2,1,0:T(8,128)(2,1)}, u32[]{:S(2)}) copy-start(bf16[128,8,128]{2,1,0:T(8,128)(2,1)} %get-tuple-element.11) | copy-start | bytes 786436
